TPU v7x, 256 devices: a whole 4x4x8 slice. The times are simulated.
256 devices in a mesh: expert: 32 (over z, y), loop: 8 (over x, core).
Axes of the slice: x: 4, y: 4, z: 8, core: 2. Of those that a mesh axis runs over, the one named last changes fastest.
Arguments:
- tokens: bfloat16 [4096, 5120], P('expert', 'loop'), may hold values from -6 to 6
- routes: int32 [4096, 6], P('expert'), may hold values from 0 to 31, all different within a row; in each aligned block of 128 rows (0 to 127, 128 to 255, ...) at most 32 rows name the same one
- route_weights: float32 [4096, 6], P('expert'), may hold values from 0.1 to 1
- gate_w: bfloat16 [32, 1536, 5120], P('expert', 'loop'), may hold values from -0.078125 to 0.078125
- up_w: bfloat16 [32, 1536, 5120], P('expert', 'loop'), may hold values from -0.078125 to 0.078125
- down_w: bfloat16 [32, 1536, 5120], P('expert', 'loop'), may hold values from -0.15625 to 0.15625
- shared_gate: bfloat16 [1536, 5120], P('loop'), may hold values from -0.078125 to 0.078125
- shared_up: bfloat16 [1536, 5120], P('loop'), may hold values from -0.078125 to 0.078125
- shared_down: bfloat16 [1536, 5120], P('loop'), may hold values from -0.15625 to 0.15625
Outputs:
- moe_out: bfloat16 [4096, 5120], P('expert', 'loop')
Inputs may be any that keep to these rules, and one draw needn't show every extreme that they name: `routes`: within the rows of one device (aligned blocks of 128 rows) no expert is named by more than 32 rows; the 6 experts of a row differ.
All inputs are finite; a program needn't handle non-finite values.
Results may differ from a plain program's by a relative error of at most 0.02.
Values may be sent and summed in bfloat16 or wider, within the bound.
No kernel may reach another device: no remote copies, remote signals or barrier semaphores. Data moves between devices by JAX's collectives and lax.ppermute only.
A program may use at most 128 MiB of HBM per device.

v0:
```python
import jax
import jax.numpy as jnp
from jax import lax
from jax.sharding import PartitionSpec as P


def project_rows(rows, weight):
    return lax.dot_general(
        rows, weight, (((1,), (1,)), ((), ())), preferred_element_type=jnp.float32
    )


def local(tokens, routes, route_weights, gate_w, up_w, down_w, shared_gate, shared_up, shared_down):
    tok_rows = tokens.shape[0]
    top_count = routes.shape[1]
    groups = lax.axis_size("expert")
    capacity = tok_rows * top_count * 4 // (3 * groups)
    slot_total = groups * capacity
    gathered = lax.all_gather(tokens, "loop", axis=1, tiled=True)
    flat_routes = routes.reshape(-1)
    onehot = (flat_routes[:, None] == jnp.arange(groups, dtype=jnp.int32)[None, :]).astype(
        jnp.int32
    )
    before = jnp.cumsum(onehot, axis=0) - onehot
    position = jnp.sum(before * onehot, axis=1)
    slot_index = (flat_routes * capacity + position).reshape(tok_rows, top_count)
    slot_ids = jnp.arange(slot_total, dtype=jnp.int32)
    matches = slot_ids[:, None, None] == slot_index[None, :, :]
    selector = jnp.sum(matches.astype(jnp.float32), axis=2).astype(jnp.bfloat16)
    combine_w = jnp.sum(jnp.where(matches, route_weights[None, :, :], 0.0), axis=2)
    combine_high = combine_w.astype(jnp.bfloat16)
    combine_low = (combine_w - combine_high.astype(jnp.float32)).astype(jnp.bfloat16)
    shared_gate_act = project_rows(gathered, shared_gate)
    shared_up_act = project_rows(gathered, shared_up)
    shared_hidden = (jax.nn.silu(shared_gate_act) * shared_up_act).astype(jnp.bfloat16)
    w_gate = gate_w[0]
    w_up = up_w[0]
    w_down = down_w[0]
    outgoing = jnp.dot(selector, gathered, preferred_element_type=jnp.float32).astype(jnp.bfloat16)
    incoming = lax.all_to_all(outgoing, "expert", split_axis=0, concat_axis=0, tiled=True)
    gate_act = project_rows(incoming, w_gate)
    up_act = project_rows(incoming, w_up)
    hidden = (jax.nn.silu(gate_act) * up_act).astype(jnp.bfloat16)
    routed_term = jnp.einsum("fc,rf->cr", w_down, hidden, preferred_element_type=jnp.float32)
    shared_term = jnp.einsum(
        "fc,rf->cr", shared_down, shared_hidden, preferred_element_type=jnp.float32
    )
    summed = lax.psum_scatter(
        jnp.concatenate([routed_term, shared_term], axis=1).astype(jnp.bfloat16),
        "loop",
        scatter_dimension=0,
        tiled=True,
    ).astype(jnp.float32)
    expert_result = summed[:, :slot_total].astype(jnp.bfloat16)
    shared_part = summed[:, slot_total:]
    returned = lax.all_to_all(expert_result, "expert", split_axis=1, concat_axis=1, tiled=True)
    routed_part = jnp.dot(returned, combine_high, preferred_element_type=jnp.float32) + jnp.dot(
        returned, combine_low, preferred_element_type=jnp.float32
    )
    return (routed_part + shared_part).T.astype(jnp.bfloat16)


def solution(mesh):
    placed = (
        P("expert", "loop"),
        P("expert", None),
        P("expert", None),
        P("expert", "loop", None),
        P("expert", "loop", None),
        P("expert", "loop", None),
        P("loop", None),
        P("loop", None),
        P("loop", None),
    )
    return jax.shard_map(
        local, mesh=mesh, in_specs=placed, out_specs=P("expert", "loop"), check_vma=False
    )
```

profile of v0, /device:TPU:3, one launch (start us, length us, event | category | flops | bytes accessed | tf_op | source)
XLA Modules:
  0.0 481.5 jit_solution(17969575525954098838)
XLA Ops:
  6.5 0.0 copy-start
  6.5 0.0 all-gather.2.cloned.1.call-start
  6.5 0.7 all-gather.2.cloned.1.call-update
  7.3 0.8 copy.38
  8.1 0.1 eq.43
  8.2 0.1 eq.39
  8.3 1.7 reduce-window.6
  10.1 0.3 slice_reduce_fusion
  10.4 0.1 fusion.30
  10.5 0.1 reduce_sum.30
  10.6 0.1 copy.41
  10.7 0.7 multiply_add_fusion
  11.4 2.2 select_reduce_fusion
  13.6 23.9 %all-gather.2.cloned.1.call-done = bf16[128,5120]{1,0:T(8,128)(2,1)} async-done(((bf16[128,640]{1,0:T(8,128)(2,1)}), bf16[128,5120]{1,0:T(8,128)(2,1)}) %all-gather.2.cloned.1.call-update) | async-done | bytes 1310736 | tf_op jit(solution)/shard_map/all_gather | solution.py:19
  37.5 6.7 %convolution_convert_fusion = bf16[1024,5120]{1,0:T(8,128)(2,1)} fusion(bf16[128,5120]{1,0:T(8,128)(2,1)} %all-gather.2.cloned.1.call-done, bf16[1024,128]{1,0:T(8,128)(2,1)S(1)} %get-tuple-element.6), kind=kOutput, calls=%fused_computation.2 | convolution fusion | flops 1347420160 | bytes 12058624 | tf_op jit(solution)/shard_map/dot_general | solution.py:39
  44.2 0.0 copy-start.2
  44.2 9.8 %all-to-all-start = ((bf16[32,32,5120]{2,1,0:T(8,128)(2,1)}), bf16[32,32,5120]{2,1,0:T(8,128)(2,1)}, u32[]{:S(2)}, u32[]{:S(2)}) async-start(bf16[32,32,5120]{2,1,0:T(8,128)(2,1)} %bitcast.57), calls=%async_computation | async-start | bytes 20971520 | tf_op jit(solution)/shard_map/all_to_all | solution.py:40
  54.0 0.2 reduce-scatter.4.cloned.1.call-start
  54.3 0.0 copy-done.2
  54.3 2.2 fusion.40
  56.5 5.1 %fusion = bf16[5120,128]{0,1:T(8,128)(2,1)} fusion(bf16[192,5120]{1,0:T(8,128)(2,1)} %param.17, bf16[128,5120]{1,0:T(8,128)(2,1)S(1)} %copy-done.2, bf16[192,5120]{1,0:T(8,128)(2,1)} %param.16, f32[128,192]{0,1:T(8,128)S(1)} %fusion.40), kind=kOutput, calls=%fused_computation.4 | convolution fusion | flops 504119296 | bytes 6651904 | tf_op jit(solution)/shard_map/fc,rf->cr/dot_general | solution.py:45
  61.6 227.4 %all-to-all-done = bf16[32,32,5120]{2,1,0:T(8,128)(2,1)} async-done(((bf16[32,32,5120]{2,1,0:T(8,128)(2,1)}), bf16[32,32,5120]{2,1,0:T(8,128)(2,1)}, u32[]{:S(2)}, u32[]{:S(2)}) %all-to-all-start) | async-done | bytes 10485792 | tf_op jit(solution)/shard_map/all_to_all | solution.py:40
  289.0 9.0 %fusion.4 = f32[1024,192]{0,1:T(8,128)} fusion(bf16[1024,5120]{1,0:T(8,128)(2,1)} %bitcast.2, bf16[1,192,5120]{2,1,0:T(8,128)(2,1)} %param.12), kind=kOutput, calls=%fused_computation.11 | convolution fusion | flops 2013265920 | bytes 13238272 | tf_op jit(solution)/shard_map/dot_general | solution.py:8
  298.0 0.0 copy-done
  298.0 0.0 copy-start.3
  298.0 17.3 %convert_bitcast_fusion = bf16[5120,1024]{0,1:T(8,128)(2,1)} fusion(bf16[1,192,5120]{2,1,0:T(8,128)(2,1)S(1)} %copy-done, bf16[1024,5120]{1,0:T(8,128)(2,1)} %bitcast.2, bf16[1,192,5120]{2,1,0:T(8,128)(2,1)} %param.13, f32[1024,192]{0,1:T(8,128)} %fusion.4), kind=kOutput, calls=%fused_computation.1 | convolution fusion | flops 4032954368 | bytes 25690112 | tf_op jit(solution)/shard_map/fc,rf->cr/dot_general | solution.py:44
  315.3 0.0 copy-done.3
  315.3 12.7 %pad_maximum_fusion = bf16[5120,1152]{0,1:T(8,128)(2,1)} fusion(bf16[5120,128]{0,1:T(8,128)(2,1)S(1)} %copy-done.3, bf16[5120,1024]{0,1:T(8,128)(2,1)} %convert_bitcast_fusion), kind=kLoop, calls=%fused_computation | loop fusion | flops 23592960 | bytes 23592960 | tf_op jit(solution)/shard_map/concatenate | solution.py:49
  328.1 15.3 %copy.44 = bf16[5120,1152]{1,0:T(8,128)(2,1)} copy(bf16[5120,1152]{0,1:T(8,128)(2,1)} %pad_maximum_fusion) | data formatting | bytes 23592960
  343.3 0.0 reduce-scatter.4.cloned.1.call-update
  343.4 82.0 %reduce-scatter.4.cloned.1.call-done = bf16[640,1152]{1,0:T(8,128)(2,1)} async-done(((bf16[5120,1152]{1,0:T(8,128)(2,1)}), bf16[640,1152]{1,0:T(8,128)(2,1)}) %reduce-scatter.4.cloned.1.call-update) | async-done | bytes 1474576 | tf_op jit(solution)/shard_map/reduce_scatter | solution.py:48
  425.4 0.0 slice-start
  425.4 1.3 slice-done
  426.7 0.7 copy.46
  427.4 0.0 copy-start.5
  427.4 0.0 copy-start.4
  427.5 45.3 %all_to_all.24 = bf16[640,32,32]{0,2,1:T(8,128)(2,1)S(1)} all-to-all(bf16[640,32,32]{0,2,1:T(8,128)(2,1)S(1)} %bitcast.60), channel_id=1, replica_groups=mesh['expert'=32,'loop'=8] {'expert'}, dimensions={1} | all-to-all | bytes 2621440 | tf_op jit(solution)/shard_map/all_to_all | solution.py:56
  472.7 0.0 copy-start.1
  472.7 0.0 copy-done.5
  472.7 0.5 fusion.26
  473.3 0.0 copy-done.4
  473.3 0.5 fusion.16
  473.8 0.8 copy.43
  474.6 0.0 copy-done.1
  (2 shorter events, 0.0 us)
Async XLA Ops:
  6.5 291.4 %copy-start = (bf16[1,192,5120]{2,1,0:T(8,128)(2,1)S(1)}, bf16[1,192,5120]{2,1,0:T(8,128)(2,1)}, u32[]{:S(2)}) copy-start(bf16[1,192,5120]{2,1,0:T(8,128)(2,1)} %param.14) | copy-start | bytes 5898244
  6.5 31.0 %all-gather.2.cloned.1.call-start = ((), (), s32[]{:S(2)}) async-start(), calls=%async_computation.3 | async-start | bytes 1474560 | tf_op jit(solution)/shard_map/all_gather | solution.py:19
  44.2 10.1 %copy-start.2 = (bf16[128,5120]{1,0:T(8,128)(2,1)S(1)}, bf16[128,5120]{1,0:T(8,128)(2,1)}, u32[]{:S(2)}) copy-start(bf16[128,5120]{1,0:T(8,128)(2,1)} %all-gather.2.cloned.1.call-done) | copy-start | bytes 3932164
  44.2 244.8 %all-to-all-start = ((bf16[32,32,5120]{2,1,0:T(8,128)(2,1)}), bf16[32,32,5120]{2,1,0:T(8,128)(2,1)}, u32[]{:S(2)}, u32[]{:S(2)}) async-start(bf16[32,32,5120]{2,1,0:T(8,128)(2,1)} %bitcast.57), calls=%async_computation | async-start | bytes 20971520 | tf_op jit(solution)/shard_map/all_to_all | solution.py:40
  54.0 371.4 %reduce-scatter.4.cloned.1.call-start = ((), (), s32[]{:S(2)}) async-start(), calls=%async_computation.4 | async-start | bytes 13271040 | tf_op jit(solution)/shard_map/reduce_scatter | solution.py:48
  298.0 17.3 %copy-start.3 = (bf16[5120,128]{0,1:T(8,128)(2,1)S(1)}, bf16[5120,128]{0,1:T(8,128)(2,1)}, u32[]{:S(2)}) copy-start(bf16[5120,128]{0,1:T(8,128)(2,1)} %fusion) | copy-start | bytes 3932164
  425.4 1.3 slice-start
  427.4 45.3 %copy-start.5 = (f32[1024,128]{1,0:T(8,128)S(1)}, f32[1024,128]{1,0:T(8,128)}, u32[]{:S(2)}) copy-start(f32[1024,128]{1,0:T(8,128)} %get-tuple-element.5) | copy-start | bytes 1572868
  427.4 45.8 %copy-start.4 = (bf16[640,1152]{1,0:T(8,128)(2,1)S(1)}, bf16[640,1152]{1,0:T(8,128)(2,1)}, u32[]{:S(2)}) copy-start(bf16[640,1152]{1,0:T(8,128)(2,1)} %reduce-scatter.4.cloned.1.call-done) | copy-start | bytes 4423684
  472.7 1.9 copy-start.1
Sparse Core Ops, SparseCore 0:
  9.2 28.2 all-gather.1
  343.5 81.8 reduce-scatter.3
where the time goes:
time: 482 us; the launch traced here: 481 us
  waiting for transfers between devices  334 us (69%)
  blocking collectives  45.3 us (9%)
  matrix products  41.4 us (9%)
  local copies, waits for them, and re-layouts  19.6 us (4%)
  other arithmetic  17.5 us (4%)
  between operations  13.5 us (3%)
  starting transfers between devices  10 us (2%)
    all_to_all x1, waiting for transfers between devices, local(): lax.all_to_all(outgoing, 'expert', split_axis=0, concat_axis=0, tiled=True)  227 us
    reduce_scatter x1, waiting for transfers between devices, local(): lax.psum_scatter(jnp.concatenate([routed_term, shared_term], axis=1).asty...  82 us
    all_to_all x1, blocking collectives, local(): lax.all_to_all(expert_result, 'expert', split_axis=1, concat_axis=1, tile...  45.3 us
    all_gather x1, waiting for transfers between devices, local(): gathered = lax.all_gather(tokens, 'loop', axis=1, tiled=True)  23.9 us
    dot_general x1, matrix products, local(): jnp.einsum('fc,rf->cr', w_down, hidden, preferred_element_type=jnp.float32)  17.3 us
    unnamed x15, local copies, waits for them, and re-layouts  16.8 us
    concatenate x1, other arithmetic, local(): jnp.concatenate([routed_term, shared_term], axis=1).astype(jnp.bfloat16)  12.7 us
    dot_general x2, matrix products, project_rows(): lax.dot_general(rows, weight, (((1,), (1,)), ((), ())), preferred_element...  11.2 us
  transfers between devices with their start and end apart: 3, of which 3 were waited for; matrix products, arithmetic and copies ran while one was open for 3% of the time, Pallas kernels for 0%

commit v1 on v0

--- a/solution.py
+++ b/solution.py
@@ -53,7 +53,9 @@
     ).astype(jnp.float32)
     expert_result = summed[:, :slot_total].astype(jnp.bfloat16)
     shared_part = summed[:, slot_total:]
-    returned = lax.all_to_all(expert_result, "expert", split_axis=1, concat_axis=1, tiled=True)
+    shards = jnp.split(expert_result, lax.axis_size("expert"), axis=1)
+    received = lax.all_to_all(jnp.stack(shards), "expert", 0, 0)
+    returned = jnp.concatenate(received, axis=1)
     routed_part = jnp.dot(returned, combine_high, preferred_element_type=jnp.float32) + jnp.dot(
         returned, combine_low, preferred_element_type=jnp.float32
     )

time: 482 us -> 535 us (1.11)
  local copies, waits for them, and re-layouts: 19.6 us -> 69.9 us
    unnamed x15 -> x107, local copies, waits for them, and re-layouts: 16.8 us -> 63 us
where the time goes in v1:
time: 535 us; the launch traced here: 533 us
  waiting for transfers between devices  334 us (62%)
  local copies, waits for them, and re-layouts  69.9 us (13%)
  blocking collectives  45.2 us (8%)
  matrix products  42.2 us (8%)
  other arithmetic  17.5 us (3%)
  between operations  13.7 us (3%)
  starting transfers between devices  9.86 us (2%)
    all_to_all x1, waiting for transfers between devices, local(): lax.all_to_all(outgoing, 'expert', split_axis=0, concat_axis=0, tiled=True)  228 us
    reduce_scatter x1, waiting for transfers between devices, local(): lax.psum_scatter(jnp.concatenate([routed_term, shared_term], axis=1).asty...  82 us
    unnamed x107, local copies, waits for them, and re-layouts  63 us
    all_to_all x1, blocking collectives, local(): received = lax.all_to_all(jnp.stack(shards), 'expert', 0, 0)  45.2 us
    all_gather x1, waiting for transfers between devices, local(): gathered = lax.all_gather(tokens, 'loop', axis=1, tiled=True)  24 us
    dot_general x1, matrix products, local(): jnp.einsum('fc,rf->cr', w_down, hidden, preferred_element_type=jnp.float32)  17.5 us
    concatenate x1, other arithmetic, local(): jnp.concatenate([routed_term, shared_term], axis=1).astype(jnp.bfloat16)  12.7 us
    dot_general x2, matrix products, project_rows(): lax.dot_general(rows, weight, (((1,), (1,)), ((), ())), preferred_element...  11.2 us
  transfers between devices with their start and end apart: 3, of which 3 were waited for; matrix products, arithmetic and copies ran while one was open for 3% of the time, Pallas kernels for 0%

profile of v1, /device:TPU:3, one launch (start us, length us, event | category | flops | bytes accessed | tf_op | source)
XLA Modules:
  0.0 532.7 jit_solution(4161392724276874686)
XLA Ops:
  7.3 0.8 copy.38
  8.3 1.7 reduce-window.6
  11.4 2.2 select_reduce_fusion
  13.6 24.0 %all-gather.2.cloned.1.call-done = bf16[128,5120]{1,0:T(8,128)(2,1)} async-done(((bf16[128,640]{1,0:T(8,128)(2,1)}), bf16[128,5120]{1,0:T(8,128)(2,1)}) %all-gather.2.cloned.1.call-update) | async-done | bytes 1310736 | tf_op jit(solution)/shard_map/all_gather | solution.py:19
  37.5 6.7 %convolution_convert_fusion = bf16[1024,5120]{1,0:T(8,128)(2,1)} fusion(bf16[128,5120]{1,0:T(8,128)(2,1)} %all-gather.2.cloned.1.call-done, bf16[1024,128]{1,0:T(8,128)(2,1)S(1)} %get-tuple-element.6), kind=kOutput, calls=%fused_computation.2 | convolution fusion | flops 1347420160 | bytes 12058624 | tf_op jit(solution)/shard_map/dot_general | solution.py:39
  44.2 9.8 %all-to-all-start = ((bf16[32,32,5120]{2,1,0:T(8,128)(2,1)}), bf16[32,32,5120]{2,1,0:T(8,128)(2,1)}, u32[]{:S(2)}, u32[]{:S(2)}) async-start(bf16[32,32,5120]{2,1,0:T(8,128)(2,1)} %bitcast.122), calls=%async_computation | async-start | bytes 20971520 | tf_op jit(solution)/shard_map/all_to_all | solution.py:40
  54.1 2.2 fusion.42
  56.3 5.1 fusion
  61.4 227.6 %all-to-all-done = bf16[32,32,5120]{2,1,0:T(8,128)(2,1)} async-done(((bf16[32,32,5120]{2,1,0:T(8,128)(2,1)}), bf16[32,32,5120]{2,1,0:T(8,128)(2,1)}, u32[]{:S(2)}, u32[]{:S(2)}) %all-to-all-start) | async-done | bytes 10485792 | tf_op jit(solution)/shard_map/all_to_all | solution.py:40
  289.0 9.0 %fusion.4 = f32[1024,192]{0,1:T(8,128)} fusion(bf16[1024,5120]{1,0:T(8,128)(2,1)} %bitcast.2, bf16[1,192,5120]{2,1,0:T(8,128)(2,1)} %param.12), kind=kOutput, calls=%fused_computation.11 | convolution fusion | flops 2013265920 | bytes 13238272 | tf_op jit(solution)/shard_map/dot_general | solution.py:8
  298.0 17.5 %convert_bitcast_fusion = bf16[5120,1024]{0,1:T(8,128)(2,1)} fusion(bf16[1,192,5120]{2,1,0:T(8,128)(2,1)S(1)} %copy-done, bf16[1024,5120]{1,0:T(8,128)(2,1)} %bitcast.2, bf16[1,192,5120]{2,1,0:T(8,128)(2,1)} %param.13, f32[1024,192]{0,1:T(8,128)} %fusion.4), kind=kOutput, calls=%fused_computation.1 | convolution fusion | flops 4032954368 | bytes 25690112 | tf_op jit(solution)/shard_map/fc,rf->cr/dot_general | solution.py:44
  315.5 12.7 %pad_maximum_fusion = bf16[5120,1152]{0,1:T(8,128)(2,1)} fusion(bf16[5120,128]{0,1:T(8,128)(2,1)S(1)} %copy-done.4, bf16[5120,1024]{0,1:T(8,128)(2,1)} %convert_bitcast_fusion), kind=kLoop, calls=%fused_computation | loop fusion | flops 23592960 | bytes 23592960 | tf_op jit(solution)/shard_map/concatenate | solution.py:49
  328.2 15.7 %copy.44 = bf16[5120,1152]{1,0:T(8,128)(2,1)} copy(bf16[5120,1152]{0,1:T(8,128)(2,1)} %pad_maximum_fusion) | data formatting | bytes 23592960
  343.9 82.0 %reduce-scatter.4.cloned.1.call-done = bf16[640,1152]{1,0:T(8,128)(2,1)} async-done(((bf16[5120,1152]{1,0:T(8,128)(2,1)}), bf16[640,1152]{1,0:T(8,128)(2,1)}) %reduce-scatter.4.cloned.1.call-update) | async-done | bytes 1474576 | tf_op jit(solution)/shard_map/reduce_scatter | solution.py:48
  425.9 2.3 fusion.41
  428.3 0.7 copy.58
  429.0 0.7 copy.57
  429.7 0.7 copy.56
  430.5 0.7 copy.55
  431.2 0.7 copy.54
  431.9 0.7 copy.53
  432.7 0.7 copy.52
  433.4 0.7 copy.51
  434.1 0.7 copy.50
  434.9 0.7 copy.49
  435.6 0.7 copy.48
  436.3 0.7 copy.47
  437.2 2.1 fusion.40
  439.3 1.0 copy.77
  440.3 1.0 copy.76
  441.4 1.6 copy.75
  443.0 1.6 copy.74
  444.7 1.6 copy.73
  446.3 1.6 copy.72
  447.9 1.6 copy.71
  449.6 1.6 copy.70
  451.2 1.6 copy.69
  452.9 1.6 copy.68
  454.5 1.6 copy.67
  456.1 1.6 copy.66
  457.8 1.6 copy.65
  459.4 1.6 copy.64
  461.1 1.7 copy.63
  462.7 0.7 copy.62
  463.5 0.7 copy.61
  464.2 0.7 copy.60
  465.0 0.7 copy.59
  465.7 0.8 constant_dynamic-update-slice_fusion.30
  466.5 0.8 constant_dynamic-update-slice_fusion.29
  467.3 0.8 constant_dynamic-update-slice_fusion.28
  468.1 0.8 constant_dynamic-update-slice_fusion.27
  468.9 0.8 constant_dynamic-update-slice_fusion.26
  469.7 0.8 constant_dynamic-update-slice_fusion.25
  470.4 0.8 constant_dynamic-update-slice_fusion.24
  471.2 0.8 constant_dynamic-update-slice_fusion.23
  472.0 0.8 constant_dynamic-update-slice_fusion.22
  472.8 0.8 constant_dynamic-update-slice_fusion.21
  473.6 0.8 constant_dynamic-update-slice_fusion.18
  474.4 0.8 constant_dynamic-update-slice_fusion.17
  475.2 0.8 constant_dynamic-update-slice_fusion.16
  476.0 0.8 constant_dynamic-update-slice_fusion.15
  477.2 45.2 %all_to_all.17 = bf16[32,640,32]{1,2,0:T(8,128)(2,1)S(1)} all-to-all(bf16[32,640,32]{1,2,0:T(8,128)(2,1)S(1)} %constant_dynamic-update-slice_fusion), channel_id=1, replica_groups=mesh['expert'=32,'loop'=8] {'expert'}, dimensions={0} | all-to-all | bytes 2621440 | tf_op jit(solution)/shard_map/all_to_all | solution.py:57
  522.9 1.2 fusion.16
  524.2 1.7 copy.43
  (75 shorter events, 3.3 us)
Async XLA Ops:
  6.5 291.5 %copy-start = (bf16[1,192,5120]{2,1,0:T(8,128)(2,1)S(1)}, bf16[1,192,5120]{2,1,0:T(8,128)(2,1)}, u32[]{:S(2)}) copy-start(bf16[1,192,5120]{2,1,0:T(8,128)(2,1)} %param.14) | copy-start | bytes 5898244
  6.5 31.0 %all-gather.2.cloned.1.call-start = ((), (), s32[]{:S(2)}) async-start(), calls=%async_computation.3 | async-start | bytes 1474560 | tf_op jit(solution)/shard_map/all_gather | solution.py:19
  44.2 9.9 %copy-start.3 = (bf16[128,5120]{1,0:T(8,128)(2,1)S(1)}, bf16[128,5120]{1,0:T(8,128)(2,1)}, u32[]{:S(2)}) copy-start(bf16[128,5120]{1,0:T(8,128)(2,1)} %all-gather.2.cloned.1.call-done) | copy-start | bytes 3932164
  44.2 244.8 %all-to-all-start = ((bf16[32,32,5120]{2,1,0:T(8,128)(2,1)}), bf16[32,32,5120]{2,1,0:T(8,128)(2,1)}, u32[]{:S(2)}, u32[]{:S(2)}) async-start(bf16[32,32,5120]{2,1,0:T(8,128)(2,1)} %bitcast.122), calls=%async_computation | async-start | bytes 20971520 | tf_op jit(solution)/shard_map/all_to_all | solution.py:40
  54.0 371.9 %reduce-scatter.4.cloned.1.call-start = ((), (), s32[]{:S(2)}) async-start(), calls=%async_computation.4 | async-start | bytes 13271040 | tf_op jit(solution)/shard_map/reduce_scatter | solution.py:48
  298.0 17.5 %copy-start.4 = (bf16[5120,128]{0,1:T(8,128)(2,1)S(1)}, bf16[5120,128]{0,1:T(8,128)(2,1)}, u32[]{:S(2)}) copy-start(bf16[5120,128]{0,1:T(8,128)(2,1)} %fusion) | copy-start | bytes 3932164
  429.0 8.2 %copy-start.2 = (bf16[640,1152]{1,0:T(8,128)(2,1)S(1)}, bf16[640,1152]{1,0:T(8,128)(2,1)}, u32[]{:S(2)}) copy-start(bf16[640,1152]{1,0:T(8,128)(2,1)} %reduce-scatter.4.cloned.1.call-done) | copy-start | bytes 4423684
  463.5 10.2 %copy-start.8 = (bf16[640,32]{0,1:T(8,128)(2,1)S(1)}, bf16[640,32]{0,1:T(8,128)(2,1)}, u32[]{:S(2)}) copy-start(bf16[640,32]{0,1:T(8,128)(2,1)} %copy.57) | copy-start | bytes 122884
  463.5 10.2 %copy-start.6 = (bf16[640,32]{0,1:T(8,128)(2,1)S(1)}, bf16[640,32]{0,1:T(8,128)(2,1)}, u32[]{:S(2)}) copy-start(bf16[640,32]{0,1:T(8,128)(2,1)} %copy.58) | copy-start | bytes 122884
  464.2 12.8 %copy-start.13 = (bf16[640,32]{0,1:T(8,128)(2,1)S(1)}, bf16[640,32]{0,1:T(8,128)(2,1)}, u32[]{:S(2)}) copy-start(bf16[640,32]{0,1:T(8,128)(2,1)} %copy.70) | copy-start | bytes 122884
  464.2 12.8 %copy-start.12 = (bf16[640,32]{0,1:T(8,128)(2,1)S(1)}, bf16[640,32]{0,1:T(8,128)(2,1)}, u32[]{:S(2)}) copy-start(bf16[640,32]{0,1:T(8,128)(2,1)} %copy.71) | copy-start | bytes 122884
  464.2 12.9 %copy-start.11 = (bf16[640,32]{0,1:T(8,128)(2,1)S(1)}, bf16[640,32]{0,1:T(8,128)(2,1)}, u32[]{:S(2)}) copy-start(bf16[640,32]{0,1:T(8,128)(2,1)} %copy.72) | copy-start | bytes 122884
  464.2 12.9 %copy-start.10 = (bf16[640,32]{0,1:T(8,128)(2,1)S(1)}, bf16[640,32]{0,1:T(8,128)(2,1)}, u32[]{:S(2)}) copy-start(bf16[640,32]{0,1:T(8,128)(2,1)} %copy.73) | copy-start | bytes 122884
  464.2 12.9 %copy-start.9 = (bf16[640,32]{0,1:T(8,128)(2,1)S(1)}, bf16[640,32]{0,1:T(8,128)(2,1)}, u32[]{:S(2)}) copy-start(bf16[640,32]{0,1:T(8,128)(2,1)} %copy.74) | copy-start | bytes 122884
  464.2 12.9 %copy-start.7 = (bf16[640,32]{0,1:T(8,128)(2,1)S(1)}, bf16[640,32]{0,1:T(8,128)(2,1)}, u32[]{:S(2)}) copy-start(bf16[640,32]{0,1:T(8,128)(2,1)} %copy.75) | copy-start | bytes 122884
  465.0 11.9 %copy-start.17 = (bf16[640,32]{0,1:T(8,128)(2,1)S(1)}, bf16[640,32]{0,1:T(8,128)(2,1)}, u32[]{:S(2)}) copy-start(bf16[640,32]{0,1:T(8,128)(2,1)} %copy.66) | copy-start | bytes 122884
  465.0 11.9 %copy-start.16 = (bf16[640,32]{0,1:T(8,128)(2,1)S(1)}, bf16[640,32]{0,1:T(8,128)(2,1)}, u32[]{:S(2)}) copy-start(bf16[640,32]{0,1:T(8,128)(2,1)} %copy.67) | copy-start | bytes 122884
  465.0 12.0 %copy-start.15 = (bf16[640,32]{0,1:T(8,128)(2,1)S(1)}, bf16[640,32]{0,1:T(8,128)(2,1)}, u32[]{:S(2)}) copy-start(bf16[640,32]{0,1:T(8,128)(2,1)} %copy.68) | copy-start | bytes 122884
  465.0 12.0 %copy-start.14 = (bf16[640,32]{0,1:T(8,128)(2,1)S(1)}, bf16[640,32]{0,1:T(8,128)(2,1)}, u32[]{:S(2)}) copy-start(bf16[640,32]{0,1:T(8,128)(2,1)} %copy.69) | copy-start | bytes 122884
  465.7 11.1 %copy-start.20 = (bf16[640,32]{0,1:T(8,128)(2,1)S(1)}, bf16[640,32]{0,1:T(8,128)(2,1)}, u32[]{:S(2)}) copy-start(bf16[640,32]{0,1:T(8,128)(2,1)} %copy.63) | copy-start | bytes 122884
  465.7 11.1 %copy-start.19 = (bf16[640,32]{0,1:T(8,128)(2,1)S(1)}, bf16[640,32]{0,1:T(8,128)(2,1)}, u32[]{:S(2)}) copy-start(bf16[640,32]{0,1:T(8,128)(2,1)} %copy.64) | copy-start | bytes 122884
  465.7 11.1 %copy-start.18 = (bf16[640,32]{0,1:T(8,128)(2,1)S(1)}, bf16[640,32]{0,1:T(8,128)(2,1)}, u32[]{:S(2)}) copy-start(bf16[640,32]{0,1:T(8,128)(2,1)} %copy.65) | copy-start | bytes 122884
  477.2 45.2 %copy-start.5 = (f32[1024,128]{1,0:T(8,128)S(1)}, f32[1024,128]{1,0:T(8,128)}, u32[]{:S(2)}) copy-start(f32[1024,128]{1,0:T(8,128)} %get-tuple-element.5) | copy-start | bytes 1572868
  522.4 3.5 copy-start.1
Sparse Core Ops, SparseCore 0:
  9.2 28.2 all-gather.1
  344.0 81.8 reduce-scatter.3
